TPU v7x, 512 devices: a whole 4x4x16 slice. The times are simulated.
512 devices in a mesh: aux: 64 (over x, z), pair: 8 (over y, core).
Axes of the slice: x: 4, y: 4, z: 16, core: 2. Of those that a mesh axis runs over, the one named last changes fastest.
Arguments:
- three_center: bfloat16 [512, 64, 1024], P('aux', 'pair'), may hold values from -6 to 6
- tile_live: int32 [64, 64], P('aux', 'pair'), may hold values from 0 to 1
- pair_atoms: int32 [64], replicated, may hold values from 0 to 63, each once
- green_occ: bfloat16 [256, 256], replicated, may hold values from -0.375 to 0.375
- green_vir: bfloat16 [256, 256], replicated, may hold values from -0.375 to 0.375
- screened: bfloat16 [512, 40], P('aux'), may hold values from -1 to 1
Outputs:
- polarizability: float32 [512, 40], P('aux', 'pair')
- self_energy: float32 [64, 1024], P('pair')
Inputs may be any that keep to these rules, and one draw needn't show every extreme that they name: `pair_atoms`: a permutation of the 64 atom pairs.
All inputs are finite; a program needn't handle non-finite values.
Results may differ from a plain program's by a relative error of at most 0.0043.
Values may be sent and summed in bfloat16 or wider, within the bound.
A program may use at most 64 MiB of HBM per device.

v0:
```python
import math
import jax
import jax.numpy as jnp
from jax import lax
from jax.sharding import PartitionSpec as P

OA = 32
NAT = 8
REACH = 2


def shifted(value, axis, steps):
    count = lax.axis_size(axis)
    initial, last = (max(0, -steps), min(count, count - steps))
    return lax.ppermute(value, axis, [(source, source + steps) for source in range(initial, last)])


def side_by_side(arrays, axis, split_dim, concat_dim, along):
    ends, at = ([], 0)
    for a in arrays[:-1]:
        at += a.shape[along]
        ends.append(at)
    both = jnp.concatenate(arrays, axis=along)
    return tuple(
        jnp.split(
            lax.all_to_all(both, axis, split_axis=split_dim, concat_axis=concat_dim, tiled=True),
            ends,
            axis=along,
        )
    )


def in_blocks(array, dim, peers):
    before, after = (array.shape[:dim], array.shape[dim + 1 :])
    return jnp.moveaxis(array.reshape(*before, peers, -1, *after), dim, 0)


def summed_on_arrival(array, axis, dim):
    peers = lax.axis_size(axis)
    blocks = lax.all_to_all(in_blocks(array, dim, peers), axis, 0, 0, tiled=True)
    return jnp.sum(blocks, axis=0)


def from_everyone(array, axis):
    peers = lax.axis_size(axis)
    return lax.all_to_all(
        jnp.broadcast_to(array[None], (peers, *array.shape)), axis, 0, 0, tiled=True
    )


def joined_along(blocks, dim):
    shape = list(blocks.shape[1:])
    shape[dim] *= blocks.shape[0]
    return jnp.moveaxis(blocks, 0, dim).reshape(shape)


def gather_directly(array, axis, dim):
    blocks = from_everyone(array, axis)
    return joined_along(blocks, dim)


def tiles_to_matrix(tile_data, inverse):
    tile_rows = tile_data.shape[0]
    ordered = jnp.take(tile_data, inverse, axis=1)
    reshaped = ordered.reshape(tile_rows, NAT, NAT, OA, OA)
    return jnp.transpose(reshaped, (0, 1, 3, 2, 4)).reshape(tile_rows, NAT * OA, NAT * OA)


def matrix_to_tiles(matrix, pair_atoms):
    tile_rows = matrix.shape[0]
    reshaped = matrix.reshape(tile_rows, NAT, OA, NAT, OA)
    ordered = jnp.transpose(reshaped, (0, 1, 3, 2, 4)).reshape(tile_rows, NAT * NAT, OA * OA)
    return jnp.take(ordered, pair_atoms, axis=1)


def neighbor_window(masked):
    pieces = []
    for offset in range(-REACH, REACH + 1):
        if offset == 0:
            pieces.append(masked)
        else:
            pieces.append(shifted(masked, "aux", -offset))
    return jnp.concatenate(pieces, axis=0)


def row_groups(orbital_form, group_fn):
    row_count = orbital_form.shape[0]
    group_size = math.gcd(row_count, 8)
    grouped = orbital_form.reshape(row_count // group_size, group_size, NAT * OA, NAT * OA)
    result = lax.map(group_fn, grouped)
    return result.reshape((row_count,) + result.shape[2:])


def all_products(orbital_form, green_occ, green_vir):

    def group_fn(row_group):
        left_half = jnp.einsum(
            "lu,plm->pum", green_occ, row_group, preferred_element_type=jnp.float32
        ).astype(jnp.bfloat16)
        return jnp.einsum(
            "pum,mv->puv", left_half, green_vir, preferred_element_type=jnp.float32
        ).astype(jnp.bfloat16)

    return row_groups(orbital_form, group_fn)


def energy_rows(mixed_tiles, occ_rows, orbital_form, tile_first):
    tile_rows, tile_count = (mixed_tiles.shape[0], mixed_tiles.shape[1])
    mixed_tiles = mixed_tiles.reshape(tile_rows, tile_count, OA, OA)
    scaled_rows = jnp.einsum(
        "qkml,kls->qkms", mixed_tiles, occ_rows, preferred_element_type=jnp.float32
    ).astype(jnp.bfloat16)
    term_sums = jnp.einsum(
        "qkms,qsn->kmn", scaled_rows, orbital_form, preferred_element_type=jnp.float32
    )
    atom_onehot = (tile_first[:, None] == jnp.arange(NAT, dtype=jnp.int32)[None, :]).astype(
        jnp.float32
    )
    return jnp.einsum("ka,kmn->amn", atom_onehot, term_sums, precision=lax.Precision.HIGHEST)


def per_device(three_center, tile_live, pair_atoms, green_occ, green_vir, screened):
    row_count, own_count = (three_center.shape[0], three_center.shape[1])
    masked = three_center * tile_live[0].astype(jnp.bfloat16)[:, None]
    inverse = jnp.argsort(pair_atoms)
    first_atom = pair_atoms // NAT
    second_atom = pair_atoms % NAT
    occ_rows = green_occ.reshape(NAT, OA, NAT * OA)
    window = neighbor_window(masked)
    flat_window = window.reshape(window.shape[0], own_count * OA * OA)
    mixed_tiles = jnp.dot(screened, flat_window, preferred_element_type=jnp.float32).astype(
        jnp.bfloat16
    )
    mixed_tiles = mixed_tiles.reshape(row_count, own_count, OA * OA)
    sub_tiles, sub_mixed = side_by_side((masked, mixed_tiles), "pair", 0, 1, 2)
    orbital_form = tiles_to_matrix(sub_tiles, inverse)
    full_form = all_products(orbital_form, green_occ, green_vir)
    products = lax.all_to_all(
        matrix_to_tiles(full_form, pair_atoms), "pair", split_axis=1, concat_axis=0, tiled=True
    )
    by_atom = energy_rows(
        sub_mixed, jnp.take(occ_rows, second_atom, axis=0), orbital_form, first_atom
    )
    chi_part = lax.dot_general(
        products.reshape(row_count, own_count * OA * OA),
        flat_window,
        (((1,), (1,)), ((), ())),
        preferred_element_type=jnp.float32,
    ) * (1.0 / (OA * NAT))
    polarizability = summed_on_arrival(chi_part, "pair", 1)
    aux_total = row_count * lax.axis_size("aux")
    sigma_scale = 1.0 / math.sqrt(aux_total * NAT * OA * NAT)
    partial_value = (
        matrix_to_tiles(by_atom.reshape(1, NAT * OA, NAT * OA), pair_atoms)[0] * -sigma_scale
    )
    columns = summed_on_arrival(partial_value, "aux", 1)
    owned_tiles = summed_on_arrival(columns, "pair", 0)
    self_energy = gather_directly(owned_tiles, "aux", 1)
    return (polarizability, self_energy)


def solution(mesh):
    placed = (P("aux", "pair", None), P("aux", "pair"), P(), P(), P(), P("aux", None))
    return jax.shard_map(
        per_device,
        mesh=mesh,
        in_specs=placed,
        out_specs=(P("aux", "pair"), P("pair", None)),
        check_vma=False,
    )
```

profile of v0, /device:TPU:1, one launch (start us, length us, event | category | flops | bytes accessed | tf_op | source)
XLA Modules:
  0.0 136.3 jit_solution(14606263857130700433)
XLA Ops:
  0.7 0.7 convert_bitcast_fusion
  1.4 1.0 broadcast_multiply_fusion
  2.3 5.7 %collective-permute-start = (bf16[8,8,1024]{2,1,0:T(8,128)(2,1)S(1)}, bf16[8,8,1024]{2,1,0:T(8,128)(2,1)S(1)}, u32[]{:S(2)}, u32[]{:S(2)}) collective-permute-start(bf16[8,8,1024]{2,1,0:T(8,128)(2,1)S(1)} %broadcast_multiply_fusion), channel_id=1, source_target_pairs={{0,16},{8,24},{16,32},{24,40},{32,48},{40,56},{48,64},{56,72},{64,... | collective-permute-start | bytes 393224 | tf_op jit(solution)/shard_map/ppermute | solution.py:15
  8.1 3.5 %collective-permute-start.1 = (bf16[8,8,1024]{2,1,0:T(8,128)(2,1)S(1)}, bf16[8,8,1024]{2,1,0:T(8,128)(2,1)S(1)}, u32[]{:S(2)}, u32[]{:S(2)}) collective-permute-start(bf16[8,8,1024]{2,1,0:T(8,128)(2,1)S(1)} %broadcast_multiply_fusion), channel_id=1, source_target_pairs={{0,8},{8,16},{16,24},{24,32},{32,40},{40,48},{48,56},{56,64},{64,7... | collective-permute-start | bytes 393224 | tf_op jit(solution)/shard_map/ppermute | solution.py:15
  11.6 1.3 collective-permute-start.2
  12.9 1.3 collective-permute-start.3
  14.2 0.7 compare_and_fusion.2
  14.9 0.7 and_select_fusion.1
  15.6 2.7 %sort.17 = (s32[64]{0:T(128)}, s32[64]{0:T(128)S(1)}) sort(s32[64]{0:T(128)} %param.10, s32[64]{0:T(128)S(1)} %iota.8), dimensions={0}, to_apply=%region_0.0 | sort | flops 384 | bytes 1024 | tf_op jit(solution)/shard_map/jit(argsort)/sort | solution.py:125
  18.3 1.0 constant_dynamic-update-slice_fusion.2
  19.4 6.0 %collective-permute-done.3 = bf16[8,8,1024]{2,1,0:T(8,128)(2,1)S(1)} collective-permute-done((bf16[8,8,1024]{2,1,0:T(8,128)(2,1)S(1)}, bf16[8,8,1024]{2,1,0:T(8,128)(2,1)S(1)}, u32[]{:S(2)}, u32[]{:S(2)}) %collective-permute-start.3) | collective-permute-done | bytes 131104 | tf_op jit(solution)/shard_map/ppermute | solution.py:15
  26.1 0.7 pad_maximum_fusion
  26.8 7.0 %all-to-all-start = ((bf16[8,8,2048]{2,1,0:T(8,128)(2,1)}), bf16[8,8,2048]{2,1,0:T(8,128)(2,1)S(1)}, u32[]{:S(2)}, u32[]{:S(2)}) async-start(bf16[8,8,2048]{2,1,0:T(8,128)(2,1)} %pad_maximum_fusion), calls=%async_computation | async-start | bytes 524288 | tf_op jit(solution)/shard_map/all_to_all | solution.py:26
  33.8 0.6 gather_fusion
  34.4 5.8 %all-to-all-done = bf16[8,8,2048]{2,1,0:T(8,128)(2,1)S(1)} async-done(((bf16[8,8,2048]{2,1,0:T(8,128)(2,1)}), bf16[8,8,2048]{2,1,0:T(8,128)(2,1)S(1)}, u32[]{:S(2)}, u32[]{:S(2)}) %all-to-all-start) | async-done | bytes 262176 | tf_op jit(solution)/shard_map/all_to_all | solution.py:26
  40.3 0.7 gather_fusion.2
  43.2 0.5 reshape.190
  43.8 0.7 gather_fusion.3
  44.8 0.5 broadcast.66
  45.3 1.4 %reduce.2 = bf16[64,1024]{1,0:T(8,128)(2,1)S(1)} reduce(bf16[64,1,1024]{2,1,0:T(2,128)(2,1)S(1)} %bitcast.84, bf16[]{:T(256)} %broadcast.66), dimensions={1}, to_apply=%bitcast.74.reduce_sub_computation | reduce | bytes 262146
  46.7 0.7 reshape.199
  47.4 4.3 %all-to-all-start.1 = ((bf16[8,2,4096]{2,1,0:T(2,128)(2,1)}), bf16[8,2,4096]{2,1,0:T(2,128)(2,1)S(1)}, u32[]{:S(2)}, u32[]{:S(2)}) async-start(bf16[8,2,4096]{2,1,0:T(2,128)(2,1)} %reshape.199), calls=%async_computation.1 | async-start | bytes 262144 | tf_op jit(solution)/shard_map/all_to_all | solution.py:138
  51.9 0.8 copy.35
  52.7 0.5 fusion
  53.2 1.3 fusion.2
  54.5 0.8 fusion.8
  55.5 0.6 copy.37
  56.1 0.5 reshape.170
  56.6 0.7 gather_fusion.1
  57.6 1.0 reshape.201
  58.6 14.4 %all-to-all-start.3 = ((f32[64,1,1024]{2,1,0:T(1,128)}), f32[64,1,1024]{2,1,0:T(1,128)S(1)}, u32[]{:S(2)}, u32[]{:S(2)}) async-start(f32[64,1,1024]{2,1,0:T(1,128)} %reshape.201), calls=%async_computation.3 | async-start | bytes 524288 | tf_op jit(solution)/shard_map/all_to_all | solution.py:40
  73.2 0.7 bitcast_reduce_fusion.1
  74.0 19.1 %all-to-all-done.3 = f32[64,1,1024]{2,1,0:T(1,128)S(1)} async-done(((f32[64,1,1024]{2,1,0:T(1,128)}), f32[64,1,1024]{2,1,0:T(1,128)S(1)}, u32[]{:S(2)}, u32[]{:S(2)}) %all-to-all-start.3) | async-done | bytes 262176 | tf_op jit(solution)/shard_map/all_to_all | solution.py:40
  93.0 0.5 broadcast.67
  93.6 1.3 reduce.3
  95.1 0.7 reshape.203
  95.8 6.2 %all-to-all-start.4 = ((f32[8,1,128]{2,1,0:T(1,128)}), f32[8,1,128]{2,1,0:T(1,128)S(1)}, u32[]{:S(2)}, u32[]{:S(2)}) async-start(f32[8,1,128]{2,1,0:T(1,128)} %reshape.203), calls=%async_computation.4 | async-start | bytes 8192 | tf_op jit(solution)/shard_map/all_to_all | solution.py:40
  102.4 0.6 copy.33
  103.0 3.5 %all-to-all-done.4 = f32[8,1,128]{2,1,0:T(1,128)S(1)} async-done(((f32[8,1,128]{2,1,0:T(1,128)}), f32[8,1,128]{2,1,0:T(1,128)S(1)}, u32[]{:S(2)}, u32[]{:S(2)}) %all-to-all-start.4) | async-done | bytes 4128 | tf_op jit(solution)/shard_map/all_to_all | solution.py:40
  106.5 3.9 %all-to-all-start.2 = ((f32[8,8,5]{2,1,0:T(8,128)}), f32[8,8,5]{2,1,0:T(8,128)S(1)}, u32[]{:S(2)}, u32[]{:S(2)}) async-start(f32[8,8,5]{2,1,0:T(8,128)} %copy.33), calls=%async_computation.2 | async-start | bytes 65536 | tf_op jit(solution)/shard_map/all_to_all | solution.py:40
  110.5 0.6 reduce.4
  111.2 0.8 reshape.205
  112.0 3.2 %all-to-all-done.2 = f32[8,8,5]{2,1,0:T(8,128)S(1)} async-done(((f32[8,8,5]{2,1,0:T(8,128)}), f32[8,8,5]{2,1,0:T(8,128)S(1)}, u32[]{:S(2)}, u32[]{:S(2)}) %all-to-all-start.2) | async-done | bytes 1312 | tf_op jit(solution)/shard_map/all_to_all | solution.py:40
  115.2 6.2 %all-to-all-start.5 = ((f32[64,1,128]{2,1,0:T(1,128)}), f32[64,1,128]{2,1,0:T(1,128)S(1)}, u32[]{:S(2)}, u32[]{:S(2)}) async-start(f32[64,1,128]{2,1,0:T(1,128)} %reshape.205), calls=%async_computation.5 | async-start | bytes 65536 | tf_op jit(solution)/shard_map/all_to_all | solution.py:46
  121.4 0.6 reduce_sum.27
  122.0 12.7 %all-to-all-done.5 = f32[64,1,128]{2,1,0:T(1,128)S(1)} async-done(((f32[64,1,128]{2,1,0:T(1,128)}), f32[64,1,128]{2,1,0:T(1,128)S(1)}, u32[]{:S(2)}, u32[]{:S(2)}) %all-to-all-start.5) | async-done | bytes 32800 | tf_op jit(solution)/shard_map/all_to_all | solution.py:46
  134.7 0.7 reduce.5
  135.6 0.8 reshape.141
  (49 shorter events, 5.0 us)
Async XLA Ops:
  0.6 33.2 %copy-start = (bf16[256,256]{1,0:T(8,128)(2,1)S(1)}, bf16[256,256]{1,0:T(8,128)(2,1)}, u32[]{:S(2)}) copy-start(bf16[256,256]{1,0:T(8,128)(2,1)} %param.11) | copy-start | bytes 393220
  0.6 25.2 %copy-start.1 = (bf16[8,40]{1,0:T(8,128)(2,1)S(1)}, bf16[8,40]{1,0:T(8,128)(2,1)}, u32[]{:S(2)}) copy-start(bf16[8,40]{1,0:T(8,128)(2,1)} %param.13) | copy-start | bytes 1924
  2.3 15.9 %collective-permute-start = (bf16[8,8,1024]{2,1,0:T(8,128)(2,1)S(1)}, bf16[8,8,1024]{2,1,0:T(8,128)(2,1)S(1)}, u32[]{:S(2)}, u32[]{:S(2)}) collective-permute-start(bf16[8,8,1024]{2,1,0:T(8,128)(2,1)S(1)} %broadcast_multiply_fusion), channel_id=1, source_target_pairs={{0,16},{8,24},{16,32},{24,40},{32,48},{40,56},{48,64},{56,72},{64,... | collective-permute-start | bytes 393224 | tf_op jit(solution)/shard_map/ppermute | solution.py:15
  8.1 10.2 %collective-permute-start.1 = (bf16[8,8,1024]{2,1,0:T(8,128)(2,1)S(1)}, bf16[8,8,1024]{2,1,0:T(8,128)(2,1)S(1)}, u32[]{:S(2)}, u32[]{:S(2)}) collective-permute-start(bf16[8,8,1024]{2,1,0:T(8,128)(2,1)S(1)} %broadcast_multiply_fusion), channel_id=1, source_target_pairs={{0,8},{8,16},{16,24},{24,32},{32,40},{40,48},{48,56},{56,64},{64,7... | collective-permute-start | bytes 393224 | tf_op jit(solution)/shard_map/ppermute | solution.py:15
  11.6 7.7 %collective-permute-start.2 = (bf16[8,8,1024]{2,1,0:T(8,128)(2,1)S(1)}, bf16[8,8,1024]{2,1,0:T(8,128)(2,1)S(1)}, u32[]{:S(2)}, u32[]{:S(2)}) collective-permute-start(bf16[8,8,1024]{2,1,0:T(8,128)(2,1)S(1)} %broadcast_multiply_fusion), channel_id=1, source_target_pairs={{8,0},{16,8},{24,16},{32,24},{40,32},{48,40},{56,48},{64,56},{72,6... | collective-permute-start | bytes 393224 | tf_op jit(solution)/shard_map/ppermute | solution.py:15
  12.9 12.5 %collective-permute-start.3 = (bf16[8,8,1024]{2,1,0:T(8,128)(2,1)S(1)}, bf16[8,8,1024]{2,1,0:T(8,128)(2,1)S(1)}, u32[]{:S(2)}, u32[]{:S(2)}) collective-permute-start(bf16[8,8,1024]{2,1,0:T(8,128)(2,1)S(1)} %broadcast_multiply_fusion), channel_id=1, source_target_pairs={{16,0},{24,8},{32,16},{40,24},{48,32},{56,40},{64,48},{72,56},{80,... | collective-permute-start | bytes 393224 | tf_op jit(solution)/shard_map/ppermute | solution.py:15
  26.8 13.5 %all-to-all-start = ((bf16[8,8,2048]{2,1,0:T(8,128)(2,1)}), bf16[8,8,2048]{2,1,0:T(8,128)(2,1)S(1)}, u32[]{:S(2)}, u32[]{:S(2)}) async-start(bf16[8,8,2048]{2,1,0:T(8,128)(2,1)} %pad_maximum_fusion), calls=%async_computation | async-start | bytes 524288 | tf_op jit(solution)/shard_map/all_to_all | solution.py:26
  40.3 2.1 %copy-start.2 = (bf16[256,256]{1,0:T(8,128)(2,1)S(1)}, bf16[256,256]{1,0:T(8,128)(2,1)}, u32[]{:S(2)}) copy-start(bf16[256,256]{1,0:T(8,128)(2,1)} %param.12) | copy-start | bytes 393220
  47.4 11.2 %all-to-all-start.1 = ((bf16[8,2,4096]{2,1,0:T(2,128)(2,1)}), bf16[8,2,4096]{2,1,0:T(2,128)(2,1)S(1)}, u32[]{:S(2)}, u32[]{:S(2)}) async-start(bf16[8,2,4096]{2,1,0:T(2,128)(2,1)} %reshape.199), calls=%async_computation.1 | async-start | bytes 262144 | tf_op jit(solution)/shard_map/all_to_all | solution.py:138
  58.6 34.4 %all-to-all-start.3 = ((f32[64,1,1024]{2,1,0:T(1,128)}), f32[64,1,1024]{2,1,0:T(1,128)S(1)}, u32[]{:S(2)}, u32[]{:S(2)}) async-start(f32[64,1,1024]{2,1,0:T(1,128)} %reshape.201), calls=%async_computation.3 | async-start | bytes 524288 | tf_op jit(solution)/shard_map/all_to_all | solution.py:40
  95.8 10.7 %all-to-all-start.4 = ((f32[8,1,128]{2,1,0:T(1,128)}), f32[8,1,128]{2,1,0:T(1,128)S(1)}, u32[]{:S(2)}, u32[]{:S(2)}) async-start(f32[8,1,128]{2,1,0:T(1,128)} %reshape.203), calls=%async_computation.4 | async-start | bytes 8192 | tf_op jit(solution)/shard_map/all_to_all | solution.py:40
  106.5 8.7 %all-to-all-start.2 = ((f32[8,8,5]{2,1,0:T(8,128)}), f32[8,8,5]{2,1,0:T(8,128)S(1)}, u32[]{:S(2)}, u32[]{:S(2)}) async-start(f32[8,8,5]{2,1,0:T(8,128)} %copy.33), calls=%async_computation.2 | async-start | bytes 65536 | tf_op jit(solution)/shard_map/all_to_all | solution.py:40
  115.2 19.5 %all-to-all-start.5 = ((f32[64,1,128]{2,1,0:T(1,128)}), f32[64,1,128]{2,1,0:T(1,128)S(1)}, u32[]{:S(2)}, u32[]{:S(2)}) async-start(f32[64,1,128]{2,1,0:T(1,128)} %reshape.205), calls=%async_computation.5 | async-start | bytes 65536 | tf_op jit(solution)/shard_map/all_to_all | solution.py:46
where the time goes:
time: 137 us; the launch traced here: 136 us
  starting transfers between devices  53.9 us (39%)
  waiting for transfers between devices  50.4 us (37%)
  local copies, waits for them, and re-layouts  15.2 us (11%)
  other arithmetic  12.3 us (9%)
  matrix products  3.47 us (3%)
    all_to_all x3, waiting for transfers between devices, summed_on_arrival(): lax.all_to_all(in_blocks(array, dim, peers), axis, 0, 0, tiled=True)  25.8 us
    all_to_all x3, starting transfers between devices, summed_on_arrival(): lax.all_to_all(in_blocks(array, dim, peers), axis, 0, 0, tiled=True)  24.6 us
    all_to_all x1, waiting for transfers between devices, from_everyone(): lax.all_to_all(jnp.broadcast_to(array[None], (peers, *array.shape)), axis...  12.7 us
    ppermute x4, starting transfers between devices, shifted(): lax.ppermute(value, axis, [(source, source + steps) for source in range(i...  11.9 us
    all_to_all x1, starting transfers between devices, side_by_side(): lax.all_to_all(both, axis, split_axis=split_dim, concat_axis=concat_dim,...  6.97 us
    all_to_all x1, starting transfers between devices, from_everyone(): lax.all_to_all(jnp.broadcast_to(array[None], (peers, *array.shape)), axis...  6.15 us
    ppermute x4, waiting for transfers between devices, shifted(): lax.ppermute(value, axis, [(source, source + steps) for source in range(i...  6.05 us
    all_to_all x1, waiting for transfers between devices, side_by_side(): lax.all_to_all(both, axis, split_axis=split_dim, concat_axis=concat_dim,...  5.85 us
  transfers between devices with their start and end apart: 10, of which 6 were waited for; matrix products, arithmetic and copies ran while one was open for 12% of the time, Pallas kernels for 0%

commit v1 on v0

--- a/solution.py
+++ b/solution.py
@@ -135,8 +135,16 @@
     sub_tiles, sub_mixed = side_by_side((masked, mixed_tiles), "pair", 0, 1, 2)
     orbital_form = tiles_to_matrix(sub_tiles, inverse)
     full_form = all_products(orbital_form, green_occ, green_vir)
-    products = lax.all_to_all(
-        matrix_to_tiles(full_form, pair_atoms), "pair", split_axis=1, concat_axis=0, tiled=True
+    products = jnp.concatenate(
+        lax.all_to_all(
+            jnp.stack(
+                jnp.split(matrix_to_tiles(full_form, pair_atoms), lax.axis_size("pair"), axis=1)
+            ),
+            "pair",
+            0,
+            0,
+        ),
+        axis=0,
     )
     by_atom = energy_rows(
         sub_mixed, jnp.take(occ_rows, second_atom, axis=0), orbital_form, first_atom

time: 137 us -> 139 us (1.015)
  local copies, waits for them, and re-layouts: 15.2 us -> 17.7 us
    unnamed x19 -> x24, local copies, waits for them, and re-layouts: 4.59 us -> 7.49 us
  transfers between devices with their start and end apart: 10 -> 10, of which waited for: 6 -> 6; matrix products, arithmetic and copies ran while one was open for 12% -> 11% of each run, Pallas kernels for 0% -> 0%
where the time goes in v1:
time: 139 us; the launch traced here: 138 us
  starting transfers between devices  53.8 us (39%)
  waiting for transfers between devices  51.3 us (37%)
  local copies, waits for them, and re-layouts  17.7 us (13%)
  other arithmetic  11 us (8%)
  matrix products  3.48 us (3%)
    all_to_all x3, waiting for transfers between devices, summed_on_arrival(): lax.all_to_all(in_blocks(array, dim, peers), axis, 0, 0, tiled=True)  26.7 us
    all_to_all x3, starting transfers between devices, summed_on_arrival(): lax.all_to_all(in_blocks(array, dim, peers), axis, 0, 0, tiled=True)  24.5 us
    all_to_all x1, waiting for transfers between devices, from_everyone(): lax.all_to_all(jnp.broadcast_to(array[None], (peers, *array.shape)), axis...  12.7 us
    ppermute x4, starting transfers between devices, shifted(): lax.ppermute(value, axis, [(source, source + steps) for source in range(i...  11.9 us
    unnamed x24, local copies, waits for them, and re-layouts  7.49 us
    all_to_all x1, starting transfers between devices, side_by_side(): lax.all_to_all(both, axis, split_axis=split_dim, concat_axis=concat_dim,...  6.97 us
    all_to_all x1, starting transfers between devices, from_everyone(): lax.all_to_all(jnp.broadcast_to(array[None], (peers, *array.shape)), axis...  6.15 us
    ppermute x4, waiting for transfers between devices, shifted(): lax.ppermute(value, axis, [(source, source + steps) for source in range(i...  6.04 us
  transfers between devices with their start and end apart: 10, of which 6 were waited for; matrix products, arithmetic and copies ran while one was open for 11% of the time, Pallas kernels for 0%

profile of v1, /device:TPU:1, one launch (start us, length us, event | category | flops | bytes accessed | tf_op | source)
XLA Modules:
  0.0 138.3 jit_solution(17545672671938203810)
XLA Ops:
  0.7 0.7 convert_bitcast_fusion
  1.4 1.0 broadcast_multiply_fusion
  2.3 5.7 %collective-permute-start = (bf16[8,8,1024]{2,1,0:T(8,128)(2,1)S(1)}, bf16[8,8,1024]{2,1,0:T(8,128)(2,1)S(1)}, u32[]{:S(2)}, u32[]{:S(2)}) collective-permute-start(bf16[8,8,1024]{2,1,0:T(8,128)(2,1)S(1)} %broadcast_multiply_fusion), channel_id=1, source_target_pairs={{0,16},{8,24},{16,32},{24,40},{32,48},{40,56},{48,64},{56,72},{64,... | collective-permute-start | bytes 393224 | tf_op jit(solution)/shard_map/ppermute | solution.py:15
  8.1 3.5 %collective-permute-start.1 = (bf16[8,8,1024]{2,1,0:T(8,128)(2,1)S(1)}, bf16[8,8,1024]{2,1,0:T(8,128)(2,1)S(1)}, u32[]{:S(2)}, u32[]{:S(2)}) collective-permute-start(bf16[8,8,1024]{2,1,0:T(8,128)(2,1)S(1)} %broadcast_multiply_fusion), channel_id=1, source_target_pairs={{0,8},{8,16},{16,24},{24,32},{32,40},{40,48},{48,56},{56,64},{64,7... | collective-permute-start | bytes 393224 | tf_op jit(solution)/shard_map/ppermute | solution.py:15
  11.6 1.3 collective-permute-start.2
  12.9 1.3 collective-permute-start.3
  14.2 0.7 and_select_fusion.1
  14.9 0.7 compare_and_fusion.2
  15.6 2.7 %sort.17 = (s32[64]{0:T(128)}, s32[64]{0:T(128)S(1)}) sort(s32[64]{0:T(128)} %param.10, s32[64]{0:T(128)S(1)} %iota.8), dimensions={0}, to_apply=%region_0.0 | sort | flops 384 | bytes 1024 | tf_op jit(solution)/shard_map/jit(argsort)/sort | solution.py:125
  18.3 1.0 constant_dynamic-update-slice_fusion.2
  19.4 6.0 %collective-permute-done.3 = bf16[8,8,1024]{2,1,0:T(8,128)(2,1)S(1)} collective-permute-done((bf16[8,8,1024]{2,1,0:T(8,128)(2,1)S(1)}, bf16[8,8,1024]{2,1,0:T(8,128)(2,1)S(1)}, u32[]{:S(2)}, u32[]{:S(2)}) %collective-permute-start.3) | collective-permute-done | bytes 131104 | tf_op jit(solution)/shard_map/ppermute | solution.py:15
  26.1 0.7 pad_maximum_fusion
  26.8 7.0 %all-to-all-start = ((bf16[8,8,2048]{2,1,0:T(8,128)(2,1)}), bf16[8,8,2048]{2,1,0:T(8,128)(2,1)S(1)}, u32[]{:S(2)}, u32[]{:S(2)}) async-start(bf16[8,8,2048]{2,1,0:T(8,128)(2,1)} %pad_maximum_fusion), calls=%async_computation | async-start | bytes 524288 | tf_op jit(solution)/shard_map/all_to_all | solution.py:26
  33.8 0.6 gather_fusion
  34.4 5.8 %all-to-all-done = bf16[8,8,2048]{2,1,0:T(8,128)(2,1)S(1)} async-done(((bf16[8,8,2048]{2,1,0:T(8,128)(2,1)}), bf16[8,8,2048]{2,1,0:T(8,128)(2,1)S(1)}, u32[]{:S(2)}, u32[]{:S(2)}) %all-to-all-start) | async-done | bytes 262176 | tf_op jit(solution)/shard_map/all_to_all | solution.py:26
  40.3 0.7 gather_fusion.2
  43.8 0.7 gather_fusion.3
  44.6 0.6 constant_dynamic-update-slice_fusion.12
  45.2 0.6 constant_dynamic-update-slice_fusion.11
  45.8 0.6 constant_dynamic-update-slice_fusion.10
  46.4 0.6 constant_dynamic-update-slice_fusion.9
  47.0 0.6 constant_dynamic-update-slice_fusion.8
  47.6 0.6 constant_dynamic-update-slice_fusion.7
  48.2 0.6 constant_dynamic-update-slice_fusion.6
  48.8 0.6 constant_dynamic-update-slice_fusion.5
  49.4 4.3 %all-to-all-start.1 = ((bf16[8,1,8,1024]{3,2,1,0:T(8,128)(2,1)}), bf16[8,1,8,1024]{3,2,1,0:T(8,128)(2,1)S(1)}, u32[]{:S(2)}, u32[]{:S(2)}) async-start(bf16[8,1,8,1024]{3,2,1,0:T(8,128)(2,1)} %constant_dynamic-update-slice_fusion.5), calls=%async_computation.1 | async-start | bytes 262144 | tf_op jit(solution)/shard_map/all_to_all | solution.py:139
  53.9 0.8 copy.33
  55.1 1.3 fusion.2
  56.4 0.8 fusion.8
  57.5 0.6 copy.35
  58.6 0.7 gather_fusion.1
  59.5 1.0 reshape.190
  60.5 14.2 %all-to-all-start.3 = ((f32[64,1,1024]{2,1,0:T(1,128)}), f32[64,1,1024]{2,1,0:T(1,128)S(1)}, u32[]{:S(2)}, u32[]{:S(2)}) async-start(f32[64,1,1024]{2,1,0:T(1,128)} %reshape.190), calls=%async_computation.3 | async-start | bytes 524288 | tf_op jit(solution)/shard_map/all_to_all | solution.py:40
  74.9 20.0 %all-to-all-done.3 = f32[64,1,1024]{2,1,0:T(1,128)S(1)} async-done(((f32[64,1,1024]{2,1,0:T(1,128)}), f32[64,1,1024]{2,1,0:T(1,128)S(1)}, u32[]{:S(2)}, u32[]{:S(2)}) %all-to-all-start.3) | async-done | bytes 262176 | tf_op jit(solution)/shard_map/all_to_all | solution.py:40
  95.4 1.3 reduce
  97.0 0.7 reshape.192
  97.7 6.3 %all-to-all-start.4 = ((f32[8,1,128]{2,1,0:T(1,128)}), f32[8,1,128]{2,1,0:T(1,128)S(1)}, u32[]{:S(2)}, u32[]{:S(2)}) async-start(f32[8,1,128]{2,1,0:T(1,128)} %reshape.192), calls=%async_computation.4 | async-start | bytes 8192 | tf_op jit(solution)/shard_map/all_to_all | solution.py:40
  104.3 0.6 copy.31
  105.0 3.5 %all-to-all-done.4 = f32[8,1,128]{2,1,0:T(1,128)S(1)} async-done(((f32[8,1,128]{2,1,0:T(1,128)}), f32[8,1,128]{2,1,0:T(1,128)S(1)}, u32[]{:S(2)}, u32[]{:S(2)}) %all-to-all-start.4) | async-done | bytes 4128 | tf_op jit(solution)/shard_map/all_to_all | solution.py:40
  108.5 3.9 %all-to-all-start.2 = ((f32[8,8,5]{2,1,0:T(8,128)}), f32[8,8,5]{2,1,0:T(8,128)S(1)}, u32[]{:S(2)}, u32[]{:S(2)}) async-start(f32[8,8,5]{2,1,0:T(8,128)} %copy.31), calls=%async_computation.2 | async-start | bytes 65536 | tf_op jit(solution)/shard_map/all_to_all | solution.py:40
  112.4 0.6 reduce.1
  113.2 0.8 reshape.194
  113.9 3.2 %all-to-all-done.2 = f32[8,8,5]{2,1,0:T(8,128)S(1)} async-done(((f32[8,8,5]{2,1,0:T(8,128)}), f32[8,8,5]{2,1,0:T(8,128)S(1)}, u32[]{:S(2)}, u32[]{:S(2)}) %all-to-all-start.2) | async-done | bytes 1312 | tf_op jit(solution)/shard_map/all_to_all | solution.py:40
  117.2 6.1 %all-to-all-start.5 = ((f32[64,1,128]{2,1,0:T(1,128)}), f32[64,1,128]{2,1,0:T(1,128)S(1)}, u32[]{:S(2)}, u32[]{:S(2)}) async-start(f32[64,1,128]{2,1,0:T(1,128)} %reshape.194), calls=%async_computation.5 | async-start | bytes 65536 | tf_op jit(solution)/shard_map/all_to_all | solution.py:46
  123.3 0.6 reduce_sum.27
  123.9 12.7 %all-to-all-done.5 = f32[64,1,128]{2,1,0:T(1,128)S(1)} async-done(((f32[64,1,128]{2,1,0:T(1,128)}), f32[64,1,128]{2,1,0:T(1,128)S(1)}, u32[]{:S(2)}, u32[]{:S(2)}) %all-to-all-start.5) | async-done | bytes 32800 | tf_op jit(solution)/shard_map/all_to_all | solution.py:46
  136.6 0.7 reduce.2
  137.5 0.8 reshape.133
  (51 shorter events, 6.7 us)
Async XLA Ops:
  0.6 33.2 %copy-start = (bf16[256,256]{1,0:T(8,128)(2,1)S(1)}, bf16[256,256]{1,0:T(8,128)(2,1)}, u32[]{:S(2)}) copy-start(bf16[256,256]{1,0:T(8,128)(2,1)} %param.11) | copy-start | bytes 393220
  0.6 25.2 %copy-start.1 = (bf16[8,40]{1,0:T(8,128)(2,1)S(1)}, bf16[8,40]{1,0:T(8,128)(2,1)}, u32[]{:S(2)}) copy-start(bf16[8,40]{1,0:T(8,128)(2,1)} %param.13) | copy-start | bytes 1924
  2.3 15.9 %collective-permute-start = (bf16[8,8,1024]{2,1,0:T(8,128)(2,1)S(1)}, bf16[8,8,1024]{2,1,0:T(8,128)(2,1)S(1)}, u32[]{:S(2)}, u32[]{:S(2)}) collective-permute-start(bf16[8,8,1024]{2,1,0:T(8,128)(2,1)S(1)} %broadcast_multiply_fusion), channel_id=1, source_target_pairs={{0,16},{8,24},{16,32},{24,40},{32,48},{40,56},{48,64},{56,72},{64,... | collective-permute-start | bytes 393224 | tf_op jit(solution)/shard_map/ppermute | solution.py:15
  8.1 10.2 %collective-permute-start.1 = (bf16[8,8,1024]{2,1,0:T(8,128)(2,1)S(1)}, bf16[8,8,1024]{2,1,0:T(8,128)(2,1)S(1)}, u32[]{:S(2)}, u32[]{:S(2)}) collective-permute-start(bf16[8,8,1024]{2,1,0:T(8,128)(2,1)S(1)} %broadcast_multiply_fusion), channel_id=1, source_target_pairs={{0,8},{8,16},{16,24},{24,32},{32,40},{40,48},{48,56},{56,64},{64,7... | collective-permute-start | bytes 393224 | tf_op jit(solution)/shard_map/ppermute | solution.py:15
  11.6 7.7 %collective-permute-start.2 = (bf16[8,8,1024]{2,1,0:T(8,128)(2,1)S(1)}, bf16[8,8,1024]{2,1,0:T(8,128)(2,1)S(1)}, u32[]{:S(2)}, u32[]{:S(2)}) collective-permute-start(bf16[8,8,1024]{2,1,0:T(8,128)(2,1)S(1)} %broadcast_multiply_fusion), channel_id=1, source_target_pairs={{8,0},{16,8},{24,16},{32,24},{40,32},{48,40},{56,48},{64,56},{72,6... | collective-permute-start | bytes 393224 | tf_op jit(solution)/shard_map/ppermute | solution.py:15
  12.9 12.5 %collective-permute-start.3 = (bf16[8,8,1024]{2,1,0:T(8,128)(2,1)S(1)}, bf16[8,8,1024]{2,1,0:T(8,128)(2,1)S(1)}, u32[]{:S(2)}, u32[]{:S(2)}) collective-permute-start(bf16[8,8,1024]{2,1,0:T(8,128)(2,1)S(1)} %broadcast_multiply_fusion), channel_id=1, source_target_pairs={{16,0},{24,8},{32,16},{40,24},{48,32},{56,40},{64,48},{72,56},{80,... | collective-permute-start | bytes 393224 | tf_op jit(solution)/shard_map/ppermute | solution.py:15
  26.8 13.5 %all-to-all-start = ((bf16[8,8,2048]{2,1,0:T(8,128)(2,1)}), bf16[8,8,2048]{2,1,0:T(8,128)(2,1)S(1)}, u32[]{:S(2)}, u32[]{:S(2)}) async-start(bf16[8,8,2048]{2,1,0:T(8,128)(2,1)} %pad_maximum_fusion), calls=%async_computation | async-start | bytes 524288 | tf_op jit(solution)/shard_map/all_to_all | solution.py:26
  40.3 2.1 %copy-start.2 = (bf16[256,256]{1,0:T(8,128)(2,1)S(1)}, bf16[256,256]{1,0:T(8,128)(2,1)}, u32[]{:S(2)}) copy-start(bf16[256,256]{1,0:T(8,128)(2,1)} %param.12) | copy-start | bytes 393220
  49.4 11.2 %all-to-all-start.1 = ((bf16[8,1,8,1024]{3,2,1,0:T(8,128)(2,1)}), bf16[8,1,8,1024]{3,2,1,0:T(8,128)(2,1)S(1)}, u32[]{:S(2)}, u32[]{:S(2)}) async-start(bf16[8,1,8,1024]{3,2,1,0:T(8,128)(2,1)} %constant_dynamic-update-slice_fusion.5), calls=%async_computation.1 | async-start | bytes 262144 | tf_op jit(solution)/shard_map/all_to_all | solution.py:139
  60.5 34.3 %all-to-all-start.3 = ((f32[64,1,1024]{2,1,0:T(1,128)}), f32[64,1,1024]{2,1,0:T(1,128)S(1)}, u32[]{:S(2)}, u32[]{:S(2)}) async-start(f32[64,1,1024]{2,1,0:T(1,128)} %reshape.190), calls=%async_computation.3 | async-start | bytes 524288 | tf_op jit(solution)/shard_map/all_to_all | solution.py:40
  97.7 10.8 %all-to-all-start.4 = ((f32[8,1,128]{2,1,0:T(1,128)}), f32[8,1,128]{2,1,0:T(1,128)S(1)}, u32[]{:S(2)}, u32[]{:S(2)}) async-start(f32[8,1,128]{2,1,0:T(1,128)} %reshape.192), calls=%async_computation.4 | async-start | bytes 8192 | tf_op jit(solution)/shard_map/all_to_all | solution.py:40
  108.5 8.7 %all-to-all-start.2 = ((f32[8,8,5]{2,1,0:T(8,128)}), f32[8,8,5]{2,1,0:T(8,128)S(1)}, u32[]{:S(2)}, u32[]{:S(2)}) async-start(f32[8,8,5]{2,1,0:T(8,128)} %copy.31), calls=%async_computation.2 | async-start | bytes 65536 | tf_op jit(solution)/shard_map/all_to_all | solution.py:40
  117.2 19.5 %all-to-all-start.5 = ((f32[64,1,128]{2,1,0:T(1,128)}), f32[64,1,128]{2,1,0:T(1,128)S(1)}, u32[]{:S(2)}, u32[]{:S(2)}) async-start(f32[64,1,128]{2,1,0:T(1,128)} %reshape.194), calls=%async_computation.5 | async-start | bytes 65536 | tf_op jit(solution)/shard_map/all_to_all | solution.py:46
